TPU v7x, 128 devices: a whole 4x4x4 slice. The times are simulated.
128 devices in a mesh: expert: 16 (over x, z), hidden: 8 (over y, core).
Axes of the slice: x: 4, y: 4, z: 4, core: 2. Of those that a mesh axis runs over, the one named last changes fastest.
Arguments:
- tokens: bfloat16 [8192, 3072], P('expert'), may hold values from -6 to 6
- out_grad: bfloat16 [8192, 3072], P('expert'), may hold values from -1.5 to 1.5
- gates: bfloat16 [8192, 8], P('expert'), may hold values from 0.19921875 to 1
- labels: int32 [8192], P('expert'), may hold values from 0 to 1, as said below
- text_picks: int32 [8, 512], replicated, may hold values from 0 to 4095, as said below
- image_picks: int32 [8, 256], replicated, may hold values from 0 to 4095, as said below
- block_mask: int32 [16, 64], P('expert', 'hidden'), may hold values 0 or 1
- w_gate: bfloat16 [16, 3072, 8192], P('expert', None, 'hidden'), may hold values from -0.109375 to 0.109375
- w_up: bfloat16 [16, 3072, 8192], P('expert', None, 'hidden'), may hold values from -0.109375 to 0.109375
- w_down: bfloat16 [16, 8192, 3072], P('expert', 'hidden'), may hold values from -0.0625 to 0.0625
Outputs:
- input_grad: bfloat16 [8192, 3072], P('expert', 'hidden')
- router_grad: bfloat16 [8192, 8], P('expert')
Inputs may be any that keep to these rules, and one draw needn't show every extreme that they name: `labels`: exactly 256 of the 512 tokens on each index of expert are text (0); the others are image (1). `text_picks`: ranks count the text tokens in order of index of expert, then position. Each row names 512 different ranks, at most 48 of them among the text tokens of one index of expert, and exactly 48 for some index. `image_picks`: ranks count the image tokens in order of index of expert, then position. Each row names 256 different ranks, at most 24 of them among the image tokens of one index of expert, and exactly 24 for some index.
All inputs are finite; a program needn't handle non-finite values. No bound on the sum of `block_mask` on one device may be relied on, other than what follows from the above.
Results may differ from a plain program's by a relative error of at most 0.02.
Values may be sent and summed in bfloat16 or wider, within the bound.
A program may use at most 128 MiB of HBM per device.

v0:
```python
import jax
import jax.numpy as jnp
from jax import lax
from jax.sharding import PartitionSpec as P

BLK = 128


def swish_parts(pre_gate):
    sigmoid_gate = jax.nn.sigmoid(pre_gate)
    return (pre_gate * sigmoid_gate, sigmoid_gate * (1.0 + pre_gate * (1.0 - sigmoid_gate)))


def place_slots(pick_ranks, my_expert, half_count, slot_count, token_order, offset):
    source = pick_ranks // half_count
    is_mine = source == my_expert
    mine_int = is_mine.astype(jnp.int32)
    earlier = jnp.cumsum(mine_int, axis=1) - mine_int
    target = jnp.where(is_mine, earlier, slot_count)
    local_rows = token_order[offset + pick_ranks % half_count]
    expert_rows = jnp.broadcast_to(
        jnp.arange(pick_ranks.shape[0], dtype=jnp.int32)[:, None], pick_ranks.shape
    )
    token_slots = (
        jnp.zeros((pick_ranks.shape[0], slot_count), jnp.int32)
        .at[expert_rows, target]
        .set(local_rows, mode="drop")
    )
    filled = (
        jnp.zeros((pick_ranks.shape[0], slot_count), jnp.bool_)
        .at[expert_rows, target]
        .set(True, mode="drop")
    )
    return (token_slots, filled)


def contract_last(left_rows, right_rows):
    return lax.dot_general(
        left_rows, right_rows, (((1,), (1,)), ((), ())), preferred_element_type=jnp.float32
    )


def body(
    tokens, out_grad, gates, labels, text_picks, image_picks, block_mask, w_gate, w_up, w_down
):
    tok_count = tokens.shape[0]
    model_width = tokens.shape[1]
    half_count = tok_count // 2
    expert_count = lax.axis_size("expert")
    hidden_count = lax.axis_size("hidden")
    modal_count = expert_count // 2
    slot_count = 3 * tok_count // (2 * expert_count)
    row_count = expert_count * slot_count
    part_width = model_width // hidden_count
    my_expert = lax.axis_index("expert")
    token_order = jnp.argsort(labels, stable=True)
    text_slots, text_filled = place_slots(
        text_picks, my_expert, half_count, slot_count, token_order, 0
    )
    image_slots, image_filled = place_slots(
        image_picks, my_expert, half_count, slot_count, token_order, half_count
    )
    token_slots = jnp.concatenate([text_slots, image_slots], 0)
    filled = jnp.concatenate([text_filled, image_filled], 0)
    column_ids = jnp.arange(expert_count, dtype=jnp.int32) % modal_count
    gate_send = jnp.where(
        filled, gates[token_slots, column_ids[:, None]], jnp.zeros((), gates.dtype)
    )
    weight_gate = w_gate[0]
    weight_up = w_up[0]
    weight_down = w_down[0]

    def pick_rows(source_rows):
        return jnp.where(
            filled[:, :, None], source_rows[token_slots], jnp.zeros((), source_rows.dtype)
        )

    token_recv, grad_recv, gate_recv = (
        lax.all_to_all(pick_rows(tokens), "expert", split_axis=0, concat_axis=0, tiled=True),
        lax.all_to_all(pick_rows(out_grad), "expert", split_axis=0, concat_axis=0, tiled=True),
        lax.all_to_all(gate_send, "expert", split_axis=0, concat_axis=0, tiled=True),
    )
    token_rows = token_recv.reshape(row_count, model_width)
    grad_rows = grad_recv.reshape(row_count, model_width)
    gate_in = jnp.dot(token_rows, weight_gate, preferred_element_type=jnp.float32)
    up_in = jnp.dot(token_rows, weight_up, preferred_element_type=jnp.float32)
    back_proj = contract_last(grad_rows, weight_down)
    block_keep = jnp.repeat(block_mask[0].astype(jnp.float32), BLK)
    swish, swish_slope = swish_parts(gate_in)
    activation = (swish * up_in * block_keep).astype(jnp.bfloat16)
    local_score = jnp.sum(activation.astype(jnp.float32) * back_proj, axis=1)
    score_total = lax.psum(local_score, "hidden")
    scale_rows = gate_recv.reshape(row_count).astype(jnp.float32)
    hidden_grad = scale_rows[:, None] * back_proj * block_keep
    gate_delta = (hidden_grad * up_in * swish_slope).astype(jnp.bfloat16)
    up_delta = (hidden_grad * swish).astype(jnp.bfloat16)
    score_send = score_total.astype(jnp.bfloat16).reshape(expert_count, slot_count)
    partial_rows = (
        contract_last(gate_delta, weight_gate) + contract_last(up_delta, weight_up)
    ).astype(jnp.bfloat16)
    partial_rows = partial_rows.reshape(expert_count, slot_count, model_width)
    back_rows, back_score = (
        lax.all_to_all(partial_rows, "expert", split_axis=0, concat_axis=0, tiled=True),
        lax.all_to_all(score_send, "expert", split_axis=0, concat_axis=0, tiled=True),
    )
    summed = lax.psum_scatter(
        back_rows.astype(jnp.float32).astype(jnp.bfloat16),
        "hidden",
        scatter_dimension=2,
        tiled=True,
    )
    grad_rows_back = summed.reshape(row_count, part_width)
    slot_flat = token_slots.reshape(row_count)
    filled_flat = filled.reshape(row_count)
    owner_table = (
        (slot_flat[None, :] == jnp.arange(tok_count, dtype=jnp.int32)[:, None])
        & filled_flat[None, :]
    ).astype(jnp.bfloat16)
    input_grad = jnp.dot(owner_table, grad_rows_back, preferred_element_type=jnp.float32).astype(
        jnp.bfloat16
    )
    column_table = (
        column_ids[:, None] == jnp.arange(modal_count, dtype=jnp.int32)[None, :]
    ).astype(jnp.bfloat16)
    score_table = (back_score[:, :, None] * column_table[:, None, :]).reshape(
        row_count, modal_count
    )
    router_grad = jnp.dot(owner_table, score_table, preferred_element_type=jnp.float32).astype(
        jnp.bfloat16
    )
    return (input_grad, router_grad)


def solution(mesh):
    placed = (
        P("expert", None),
        P("expert", None),
        P("expert", None),
        P("expert"),
        P(),
        P(),
        P("expert", "hidden"),
        P("expert", None, "hidden"),
        P("expert", None, "hidden"),
        P("expert", "hidden", None),
    )
    return jax.shard_map(
        body,
        mesh=mesh,
        in_specs=placed,
        out_specs=(P("expert", "hidden"), P("expert", None)),
        check_vma=False,
    )
```

profile of v0, /device:TPU:0, one launch (start us, length us, event | category | flops | bytes accessed | tf_op | source)
XLA Modules:
  0.0 453.6 jit_solution(12359741630690584256)
XLA Ops:
  20.1 25.9 %gather_fusion = s32[4096]{0:T(1024)S(1)} fusion(s32[512]{0:T(512)S(1)} %get-tuple-element.3, s32[4096]{0:T(1024)S(1)} %broadcast_clamp_fusion), kind=kCustom, calls=%fused_computation | custom fusion | bytes 49152 | tf_op jit(solution)/shard_map/gather | solution.py:20
  46.0 15.5 %scatter_custom_fusion = s32[384]{0:T(512)S(1)} fusion(s32[4096]{0:T(1024)S(1)} %bitcast.74, s32[4096]{0:T(1024)S(1)} %gather_fusion, s32[]{:T(128)} %constant.86.clone.1), kind=kCustom, calls=%fused_computation.106 | custom fusion | bytes 1540
  61.7 13.2 %gather_fusion.1 = s32[2048]{0:T(1024)S(1)} fusion(s32[512]{0:T(512)S(1)} %get-tuple-element.3, s32[2048]{0:T(1024)S(1)} %broadcast_clamp_fusion.1), kind=kCustom, calls=%fused_computation.1 | custom fusion | bytes 24576 | tf_op jit(solution)/shard_map/gather | solution.py:20
  74.9 8.0 %scatter_custom_fusion.1 = s32[384]{0:T(512)S(1)} fusion(s32[2048]{0:T(1024)S(1)} %bitcast.76, s32[2048]{0:T(1024)S(1)} %gather_fusion.1, s32[]{:T(128)} %constant.86.clone.1), kind=kCustom, calls=%fused_computation.104 | custom fusion | bytes 1540
  83.0 9.3 %scatter_custom_fusion.3 = pred[384]{0:T(512)(128)(4,1)S(1)} fusion(s32[2048]{0:T(1024)S(1)} %bitcast.77, pred[2048]{0:T(1024)(128)(4,1)S(1)} %broadcast.228, pred[]{:T(512)} %constant.97.clone.1), kind=kCustom, calls=%fused_computation.108 | custom fusion | bytes 385
  92.3 17.6 %scatter_custom_fusion.2 = pred[384]{0:T(512)(128)(4,1)S(1)} fusion(s32[4096]{0:T(1024)S(1)} %bitcast.75, pred[4096]{0:T(1024)(128)(4,1)S(1)} %broadcast.226, pred[]{:T(512)} %constant.97.clone.1), kind=kCustom, calls=%fused_computation.110 | custom fusion | bytes 385
  110.1 6.3 %gather_fusion.2 = bf16[768]{0:T(1024)(128)(2,1)S(1)} fusion(bf16[512,8]{0,1:T(8,128)(2,1)S(1)} %copy-done.2, s32[768]{0:T(1024)S(1)} %reshape.285), kind=kCustom, calls=%fused_computation.2 | custom fusion | bytes 9216 | tf_op jit(solution)/shard_map/gather | solution.py:67
  117.3 8.0 %all-to-all-start = ((bf16[16,1,48]{2,1,0:T(2,128)(2,1)}), bf16[16,1,48]{2,1,0:T(2,128)(2,1)S(1)}, u32[]{:S(2)}, u32[]{:S(2)}) async-start(bf16[16,1,48]{2,1,0:T(2,128)(2,1)} %copy.12), calls=%async_computation | async-start | bytes 16384 | tf_op jit(solution)/shard_map/all_to_all | solution.py:81
  125.6 5.0 %gather_fusion.4 = bf16[768,3072]{1,0:T(8,128)(2,1)} fusion(bf16[512,3072]{1,0:T(8,128)(2,1)S(1)} %copy-done, s32[1024]{0:T(1024)S(1)} %pad_clamp_fusion), kind=kCustom, calls=%fused_computation.4 | custom fusion | bytes 9440256 | tf_op jit(solution)/shard_map/gather | solution.py:75
  130.6 12.1 %gather_fusion.3 = bf16[768,3072]{1,0:T(8,128)(2,1)} fusion(bf16[512,3072]{1,0:T(8,128)(2,1)} %param.11, s32[1024]{0:T(1024)S(1)} %pad_clamp_fusion), kind=kCustom, calls=%fused_computation.3 | custom fusion | bytes 9440256 | tf_op jit(solution)/shard_map/gather | solution.py:75
  142.7 8.1 %broadcast_select_fusion.1 = (bf16[16,48,3072]{2,1,0:T(8,128)(2,1)}, bf16[16,48,3072]{2,1,0:T(8,128)(2,1)}) fusion(bf16[16,48,3072]{2,1,0:T(8,128)(2,1)} %bitcast.66, pred[16,48]{1,0:T(8,128)(4,1)S(1)} %constant_dynamic-update-slice_fusion, bf16[16,48,3072]{2,1,0:T(8,128)(2,1)} %bitcast.65), kind=kLoop, calls=%fused_computation.21 | loop fusion | flops 4718592 | bytes 18875136 | tf_op jit(solution)/shard_map/jit(_where)/select_n | solution.py:74
  150.8 63.2 %all_to_all.31 = bf16[16,48,3072]{2,1,0:T(8,128)(2,1)} all-to-all(bf16[16,48,3072]{2,1,0:T(8,128)(2,1)} %get-tuple-element.11), channel_id=1, replica_groups=mesh['expert'=16,'hidden'=8] {'expert'}, dimensions={0} | all-to-all | bytes 9437184 | tf_op jit(solution)/shard_map/all_to_all | solution.py:79
  219.2 8.7 %fusion.2 = f32[768,1024]{1,0:T(8,128)S(1)} fusion(bf16[768,3072]{1,0:T(8,128)(2,1)} %bitcast.68, bf16[1,3072,1024]{2,1,0:T(8,128)(2,1)} %param.17), kind=kOutput, calls=%fused_computation.12 | convolution fusion | flops 4831838208 | bytes 14155776 | tf_op jit(solution)/shard_map/dot_general | solution.py:85
  227.9 8.3 %fusion.6 = f32[768,1024]{1,0:T(8,128)} fusion(bf16[768,3072]{1,0:T(8,128)(2,1)S(1)} %bitcast.69, bf16[1,3072,1024]{2,1,0:T(8,128)(2,1)} %param.18), kind=kOutput, calls=%fused_computation.16 | convolution fusion | flops 4831838208 | bytes 14155776 | tf_op jit(solution)/shard_map/dot_general | solution.py:86
  236.1 42.9 %all-to-all-done.1 = bf16[16,48,3072]{2,1,0:T(8,128)(2,1)} async-done(((bf16[16,48,3072]{2,1,0:T(8,128)(2,1)}), bf16[16,48,3072]{2,1,0:T(8,128)(2,1)}, u32[]{:S(2)}, u32[]{:S(2)}) %all-to-all-start.1) | async-done | bytes 4718624 | tf_op jit(solution)/shard_map/all_to_all | solution.py:80
  279.0 9.9 %multiply_reduce_fusion = (f32[768]{0:T(1024)S(1)}, f32[768,1024]{1,0:T(8,128)S(1)}) fusion(f32[768,1024]{1,0:T(8,128)} %fusion.6, f32[1024]{0:T(1024)S(1)} %broadcast_bitcast_fusion, f32[768,1024]{1,0:T(8,128)S(1)} %fusion.2, bf16[768,3072]{1,0:T(8,128)(2,1)} %bitcast.7, bf16[1,1024,3072]{2,1,0:T(8,128)(2,1)} %param.19), kind=kOutput, calls=%fused_computation.22 | convolution fusion | flops 4839701504 | bytes 20454400 | tf_op jit(solution)/shard_map/dot_general | solution.py:38
  288.9 11.5 %fusion = f32[768,3072]{1,0:T(8,128)} fusion(bf16[1,3072,1024]{2,1,0:T(8,128)(2,1)} %param.17, f32[768,1024]{1,0:T(8,128)S(1)} %fusion.2, f32[768,1024]{1,0:T(8,128)S(1)} %copy-done.5, f32[768,1024]{1,0:T(8,128)S(1)} %get-tuple-element.13, f32[1024]{0:T(1024)S(1)} %broadcast_bitcast_fusion, f32[768]{0:T(1024)S(1)} %reshape.268), kind=kOutput, calls=%fused_computation.10 | convolution fusion | flops 4841275392 | bytes 25172992 | tf_op jit(solution)/shard_map/dot_general | solution.py:38
  300.4 10.2 %add_convert_fusion = bf16[768,3072]{1,0:T(8,128)(2,1)S(1)} fusion(f32[768,3072]{1,0:T(8,128)} %fusion, bf16[1,3072,1024]{2,1,0:T(8,128)(2,1)} %param.18, f32[768,1024]{1,0:T(8,128)S(1)} %get-tuple-element.13, f32[1024]{0:T(1024)S(1)} %broadcast_bitcast_fusion, f32[768]{0:T(1024)S(1)} %reshape.268, f32[768,1024]{1,0:T(8,128)S(1)} %fusion.2), kind=kOutput, calls=%fused_computation.9 | convolution fusion | flops 4842848256 | bytes 26745856 | tf_op jit(solution)/shard_map/dot_general | solution.py:38
  310.6 57.1 %all_to_all.32 = bf16[16,48,3072]{2,1,0:T(8,128)(2,1)} all-to-all(bf16[16,48,3072]{2,1,0:T(8,128)(2,1)S(1)} %bitcast.70), channel_id=1, replica_groups=mesh['expert'=16,'hidden'=8] {'expert'}, dimensions={0} | all-to-all | bytes 9437184 | tf_op jit(solution)/shard_map/all_to_all | solution.py:103
  367.7 14.9 %copy.14 = bf16[16,48,3072]{1,0,2:T(8,128)(2,1)} copy(bf16[16,48,3072]{2,1,0:T(8,128)(2,1)} %all_to_all.32) | data formatting | bytes 9437184
  382.7 18.1 %reshape.340 = bf16[3072,768]{1,0:T(8,128)(2,1)} reshape(bf16[3072,16,48]{2,1,0:T(8,128)(2,1)} %bitcast.64) | data formatting | bytes 9437184
  401.0 12.5 %psum.7 = bf16[768]{0:T(1024)(128)(2,1)S(1)} all-reduce(f32[768]{0:T(1024)S(1)} %get-tuple-element.12), channel_id=1, replica_groups=mesh['expert'=16,'hidden'=8] {'hidden'}, use_global_device_ids=true, to_apply=%region_11.12 | all-reduce | flops 768 | bytes 4608 | tf_op jit(solution)/shard_map/psum | solution.py:92
  418.2 7.3 %all-to-all-done.4 = bf16[16,1,48]{2,1,0:T(2,128)(2,1)S(1)} async-done(((bf16[16,1,48]{2,1,0:T(2,128)(2,1)}), bf16[16,1,48]{2,1,0:T(2,128)(2,1)S(1)}, u32[]{:S(2)}, u32[]{:S(2)}) %all-to-all-start.4) | async-done | bytes 1568 | tf_op jit(solution)/shard_map/all_to_all | solution.py:104
  426.9 11.1 %reduce-scatter.4.cloned.1.call-done = bf16[384,768]{1,0:T(8,128)(2,1)} async-done(((bf16[3072,768]{1,0:T(8,128)(2,1)}), bf16[384,768]{1,0:T(8,128)(2,1)}) %reduce-scatter.4.cloned.1.call-update) | async-done | bytes 589840
  (86 shorter events, 34.6 us)
Async XLA Ops:
  7.2 118.4 %copy-start = (bf16[512,3072]{1,0:T(8,128)(2,1)S(1)}, bf16[512,3072]{1,0:T(8,128)(2,1)}, u32[]{:S(2)}) copy-start(bf16[512,3072]{1,0:T(8,128)(2,1)} %param.10) | copy-start | bytes 9437188
  61.7 48.4 %copy-start.2 = (bf16[512,8]{0,1:T(8,128)(2,1)S(1)}, bf16[512,8]{0,1:T(8,128)(2,1)}, u32[]{:S(2)}) copy-start(bf16[512,8]{0,1:T(8,128)(2,1)} %param.12) | copy-start | bytes 24580
  117.3 33.5 %all-to-all-start = ((bf16[16,1,48]{2,1,0:T(2,128)(2,1)}), bf16[16,1,48]{2,1,0:T(2,128)(2,1)S(1)}, u32[]{:S(2)}, u32[]{:S(2)}) async-start(bf16[16,1,48]{2,1,0:T(2,128)(2,1)} %copy.12), calls=%async_computation | async-start | bytes 16384 | tf_op jit(solution)/shard_map/all_to_all | solution.py:81
  214.0 5.0 %copy-start.4 = (s32[1,8]{1,0:T(1,128)S(1)}, s32[1,8]{1,0:T(1,128)}, u32[]{:S(2)}) copy-start(s32[1,8]{1,0:T(1,128)} %param.16) | copy-start | bytes 100
  214.0 65.0 %all-to-all-start.1 = ((bf16[16,48,3072]{2,1,0:T(8,128)(2,1)}), bf16[16,48,3072]{2,1,0:T(8,128)(2,1)}, u32[]{:S(2)}, u32[]{:S(2)}) async-start(bf16[16,48,3072]{2,1,0:T(8,128)(2,1)} %get-tuple-element.10), calls=%async_computation.1 | async-start | bytes 9437184 | tf_op jit(solution)/shard_map/all_to_all | solution.py:80
  218.7 219.3 %reduce-scatter.4.cloned.1.call-start = ((), (), s32[]{:S(2)}) async-start(), calls=%async_computation.6 | async-start | bytes 5308416
  219.2 8.7 %copy-start.3 = (bf16[16,48,3072]{2,1,0:T(8,128)(2,1)S(1)}, bf16[16,48,3072]{2,1,0:T(8,128)(2,1)}, u32[]{:S(2)}) copy-start(bf16[16,48,3072]{2,1,0:T(8,128)(2,1)} %all_to_all.31) | copy-start | bytes 14155780
  279.0 9.9 %copy-start.5 = (f32[768,1024]{1,0:T(8,128)S(1)}, f32[768,1024]{1,0:T(8,128)}, u32[]{:S(2)}) copy-start(f32[768,1024]{1,0:T(8,128)} %fusion.6) | copy-start | bytes 9437188
  414.1 11.4 %all-to-all-start.4 = ((bf16[16,1,48]{2,1,0:T(2,128)(2,1)}), bf16[16,1,48]{2,1,0:T(2,128)(2,1)S(1)}, u32[]{:S(2)}, u32[]{:S(2)}) async-start(bf16[16,1,48]{2,1,0:T(2,128)(2,1)} %all_to_all.25), calls=%async_computation.4 | async-start | bytes 16384 | tf_op jit(solution)/shard_map/all_to_all | solution.py:104
  425.8 20.9 %copy-start.1 = (bf16[512,3072]{1,0:T(8,128)(2,1)S(1)}, bf16[512,3072]{1,0:T(8,128)(2,1)}, u32[]{:S(2)}) copy-start(bf16[512,3072]{1,0:T(8,128)(2,1)} %param.10) | copy-start | bytes 9437188
Sparse Core Ops, SparseCore 0:
  400.9 37.0 reduce-scatter.3
where the time goes:
time: 455 us; the launch traced here: 454 us
  local copies, waits for them, and re-layouts  155 us (34%)
  blocking collectives  133 us (29%)
  waiting for transfers between devices  61.4 us (13%)
  matrix products  51.9 us (11%)
  other arithmetic  21 us (5%)
  starting transfers between devices  16.8 us (4%)
  between operations  14.4 us (3%)
    unnamed x28, local copies, waits for them, and re-layouts  89.8 us
    all_to_all x1, blocking collectives, body(): lax.all_to_all(pick_rows(tokens), 'expert', split_axis=0, concat_axis=0,...  63.2 us
    all_to_all x1, blocking collectives, body(): lax.all_to_all(partial_rows, 'expert', split_axis=0, concat_axis=0, tiled...  57.1 us
    all_to_all x1, waiting for transfers between devices, body(): lax.all_to_all(pick_rows(out_grad), 'expert', split_axis=0, concat_axis=0...  42.9 us
    gather x2, local copies, waits for them, and re-layouts, place_slots(): local_rows = token_order[offset + pick_ranks % half_count]  39.1 us
    dot_general x3, matrix products, contract_last(): lax.dot_general(left_rows, right_rows, (((1,), (1,)), ((), ())), preferre...  31.5 us
    gather x2, local copies, waits for them, and re-layouts, pick_rows(): source_rows[token_slots]  17.1 us
    psum x1, blocking collectives, body(): score_total = lax.psum(local_score, 'hidden')  12.5 us
  transfers between devices with their start and end apart: 4, of which 3 were waited for; matrix products, arithmetic and copies ran while one was open for 10% of the time, Pallas kernels for 0%

commit v1 on v0

v1 whole, which is shorter than its diff:
```python
import jax
import jax.numpy as jnp
from jax import lax
from jax.experimental import pallas as pl
from jax.experimental.pallas import tpu as pltpu
from jax.sharding import PartitionSpec as P

MESH = pl.DeviceIdType.MESH
F32 = jnp.float32
BF16 = jnp.bfloat16

TD = 512
HALF = 256
NE = 16
EH = 8
SL = 48
SI = 24
NS = NE * SL
D = 3072
FB = 384
YB = 768
FH = 1024
RC = 256


def nt(a, b):
    return lax.dot_general(a, b, (((1,), (1,)), ((), ())), preferred_element_type=F32)


def nn(a, b):
    return jnp.dot(a, b, preferred_element_type=F32)


def iota(shape, dim):
    return lax.broadcasted_iota(jnp.int32, shape, dim)


def one(cond):
    return jnp.where(cond, 1.0, 0.0).astype(F32)


def kernel(
    tok_h, og_h, gates, labels, tpk, ipk, mask, wg_h, wu_h, wd_h,
    ig, rg,
    wg, wu, wd, cols, tri, idn, mref, smat, s2mat, gmat, omat, pmat, ptmat,
    send_t, send_i, recv, x, acc, gd, ud, stage, crecv, fstage, ustage, dstage,
    arecv, brecv, urecv, drecv, rgm, vsend, vrecv, srecv, scs, scr,
    ld_sem, w_sem, s1t, s1i, r1, sy, ry, sc, rc, ss, rs, scc, rcc, sab, rab, sud, rud,
    sv, rv, sq, rq,
):
    me = lax.axis_index("expert")
    h = lax.axis_index("hidden")
    y = lax.div(h, 2)
    c = lax.rem(h, 2)
    oc = 1 - c
    far = lax.rem(y + 2, 4)
    up = lax.rem(y + 1, 4)
    dn = lax.rem(y + 3, 4)
    kcol = lax.rem(me, EH)
    is_text = me < EH
    n_chunks = 2 - lax.div(me, EH)
    blocks = (y, far, up, dn)

    def remote(src, dst, s_sem, r_sem, **where):
        return pltpu.make_async_remote_copy(
            src_ref=src, dst_ref=dst, send_sem=s_sem, recv_sem=r_sem,
            device_id=where, device_id_type=MESH,
        )

    def colsl(core):
        return pl.ds(pl.multiple_of(core * FB, 128), FB)

    def rowsl(r):
        return pl.ds(pl.multiple_of(r * RC, RC), RC)

    loads = []
    for f, yy in enumerate((y, far)):
        fs = pl.ds(pl.multiple_of((yy * 2 + c) * FB, 128), FB)
        for a, src in enumerate((tok_h, og_h)):
            cp = pltpu.make_async_copy(
                src.at[:, fs], cols.at[f, pl.ds(a * TD, TD), :], ld_sem.at[f, a])
            cp.start()
            loads.append(cp)
    wloads = []
    for k, yy in enumerate(blocks):
        rows = pl.ds(pl.multiple_of(yy * YB, YB), YB)
        trio = [
            pltpu.make_async_copy(wg_h.at[rows, :], wg.at[rows, :], w_sem.at[k, 0]),
            pltpu.make_async_copy(wu_h.at[rows, :], wu.at[rows, :], w_sem.at[k, 1]),
            pltpu.make_async_copy(wd_h.at[:, rows], wd.at[:, rows], w_sem.at[k, 2]),
        ]
        for cp in trio:
            cp.start()
        wloads.append(trio)

    barrier = pltpu.get_barrier_semaphore()

    @pl.loop(1, NE)
    def _(k):
        pl.semaphore_signal(barrier, inc=1, device_id={"expert": lax.rem(me + k, NE)}, device_id_type=MESH)

    @pl.loop(1, 8)
    def _(k):
        pl.semaphore_signal(barrier, inc=1, device_id={"hidden": lax.rem(h + k, 8)}, device_id_type=MESH)

    r5 = iota((TD, TD), 0)
    c5 = iota((TD, TD), 1)
    tri[...] = one(r5 <= c5).astype(BF16)
    idn[...] = one(r5 == c5).astype(BF16)
    text = one(labels[...] == 0)
    lab16 = jnp.where(iota((NE, TD), 0) < EH, text, 1.0 - text)
    rank = nn(lab16.astype(BF16), tri[...])
    key = jnp.where(lab16 > 0.0, rank - 1.0, -1.0)

    def local_rank(p):
        return jnp.where(lax.shift_right_logical(p, 8) == me, (p & 255), -1).astype(F32)

    lov = jnp.concatenate([
        local_rank(tpk[...]),
        jnp.concatenate([local_rank(ipk[...]), jnp.full((EH, TD - HALF), -1.0, F32)], axis=1),
    ], axis=0)
    lov_t = nt(idn[...], lov.astype(BF16))
    rrow = iota((1, HALF), 1).astype(F32)
    for e in range(NE):
        depth = TD if e < EH else HALF
        hit = one(lov_t[:depth, e:e + 1] == rrow)
        mref[e:e + 1, :] = jnp.sum(hit, axis=0, keepdims=True)
    member = mref[...]
    slot1 = member * nn(member.astype(BF16), tri[:HALF, :HALF])
    slot1 = slot1.astype(BF16)
    rcol = iota((HALF, TD), 0).astype(F32)
    st_text = nn(slot1, one(rcol == key[0:1, :]).astype(BF16))
    st_image = nn(slot1, one(rcol == key[EH:EH + 1, :]).astype(BF16))
    st = jnp.where(iota((NE, TD), 0) < EH, st_text, st_image)
    s1 = iota((SL, TD), 0).astype(F32) + 1.0
    for e in range(EH):
        smat[e * SL:(e + 1) * SL, :] = one(st[e:e + 1, :] == s1).astype(BF16)
        im = st[EH + e:EH + e + 1, :]
        s2mat[e * SL:(e + 1) * SL, :TD] = one(im == s1).astype(BF16)
        im2 = jnp.where(im > 0.0, im + SI, -1.0)
        s2mat[e * SL:(e + 1) * SL, TD:] = one(im2 == s1).astype(BF16)

    pl.semaphore_wait(barrier, NE - 1 + 7)

    def text_copy(f, a, d):
        return remote(send_t.at[f, a, d], recv.at[f, a, me], s1t.at[f, a, d], r1.at[f, a, me], expert=d)

    def image_copy(f, d):
        return remote(send_i.at[f, d], recv.at[f, 0, me], s1i.at[f, d], r1.at[f, 0, me], expert=EH + d)

    for f in range(2):
        for a in range(2):
            loads[f * 2 + a].wait()
            t = nn(smat[...], cols[f, a * TD:(a + 1) * TD, :])
            send_t[f, a] = t.astype(BF16).reshape(EH, SL, FB)

            @pl.loop(0, EH)
            def _(k):
                d = lax.rem(me + k, EH)

                @pl.when(d != me)
                def _():
                    text_copy(f, a, d).start()

                @pl.when(d == me)
                def _():
                    recv[f, a, me] = send_t[f, a, d]

        t = nn(s2mat[...], cols[f])
        send_i[f] = t.astype(BF16).reshape(EH, SL, FB)

        @pl.loop(0, EH)
        def _(k):
            d = lax.rem(me + k, EH)

            @pl.when(EH + d != me)
            def _():
                image_copy(f, d).start()

            @pl.when(EH + d == me)
            def _():
                recv[f, 0, me] = send_i[f, d]

    jq_row = jnp.floor((iota((1, NS), 1).astype(F32) + 0.5) * (1.0 / SL))
    jr_row = iota((1, NS), 1).astype(F32) - jq_row * SL
    jq_col = jnp.floor((iota((NS, 1), 0).astype(F32) + 0.5) * (1.0 / SL))
    jr_col = iota((NS, 1), 0).astype(F32) - jq_col * SL

    def source(p):
        return lax.shift_right_logical(p, 8).astype(F32)

    src_text = source(tpk[pl.ds(kcol, 1), :])
    src_image = jnp.concatenate(
        [source(ipk[pl.ds(kcol, 1), :]), jnp.full((1, TD - HALF), 99.0, F32)], axis=1)
    src = jnp.where(is_text, src_text, src_image)
    i16 = iota((NE, 1), 0).astype(F32)
    cnt16 = jnp.sum(one(src == i16), axis=1, keepdims=True)
    off16 = jnp.sum(one(src < i16), axis=1, keepdims=True)
    spread = iota((NE, NS), 0).astype(F32) == jq_row
    cnt_row = jnp.sum(jnp.where(spread, cnt16, 0.0), axis=0, keepdims=True)
    off_row = jnp.sum(jnp.where(spread, off16, 0.0), axis=0, keepdims=True)
    for a in range(2):
        shift = (lax.div(me, EH) * (SI * a)).astype(F32)
        place = jr_row - shift
        good = jnp.where((place >= 0.0) & (place < cnt_row), off_row + place, -1.0)
        pmat[a] = one(iota((TD, NS), 0).astype(F32) == good).astype(BF16)
    cnt_col = jnp.sum(one(src == jq_col), axis=1, keepdims=True)
    off_col = jnp.sum(one(src < jq_col), axis=1, keepdims=True)
    good_col = jnp.where(jr_col < cnt_col, off_col + jr_col, -1.0)
    ptmat[...] = one(iota((NS, TD), 1).astype(F32) == good_col).astype(BF16)

    st_t = nt(idn[...], st.astype(BF16)).astype(BF16)
    st_wide = nn(st_t, one(spread).astype(BF16))
    filled = st_wide == jr_row + 1.0
    omat[...] = one(filled).astype(BF16)
    k_row = jnp.where(jq_row >= EH, jq_row - EH, jq_row)
    spread_k = one(iota((EH, NS), 0).astype(F32) == k_row).astype(BF16)
    gate_wide = nn(gates[...], spread_k)
    gmat[...] = jnp.where(filled, gate_wide, 0.0).astype(BF16)
    vrecv[EH:, 32:, :] = jnp.zeros((EH, SL - 32, FB), BF16)
    srecv[h] = jnp.zeros((1, TD), F32)

    def y_copy(a, r, way):
        ref = x.at[a, y, rowsl(r), colsl(c)]
        return remote(ref, ref, sy.at[a, r, way], ry.at[a, r, way], hidden=(up, dn)[way] * 2 + c)

    def y_wait(a, r, way):
        ref = x.at[a, (dn, up)[way], rowsl(r), colsl(c)]
        remote(ref, ref, sy.at[a, r, way], ry.at[a, r, way], hidden=(dn, up)[way] * 2 + c).wait_recv()

    def core_copy(a, k, r):
        ref = x.at[a, blocks[k], rowsl(r), colsl(c)]
        return remote(ref, ref, sc.at[a, k, r], rc.at[a, k, r], hidden=y * 2 + oc)

    def core_wait(a, k, r):
        ref = x.at[a, blocks[k], rowsl(r), colsl(oc)]
        remote(ref, ref, sc.at[a, k, r], rc.at[a, k, r], hidden=y * 2 + oc).wait_recv()

    def compact(f, a):
        aa = a * (1 - lax.div(me, EH)) if a else 0

        def await_source(s):
            @pl.when(s != me)
            def _():
                remote(send_t.at[f, a, 0], recv.at[f, aa, s], s1t.at[f, a, 0], r1.at[f, aa, s], expert=s).wait_recv()

        if a == 0:
            pl.loop(0, NE)(await_source)
        else:
            @pl.when(is_text)
            def _():
                pl.loop(0, NE)(await_source)

        @pl.loop(0, n_chunks)
        def _(r):
            got = nn(pmat[a, rowsl(r), :], recv[f, aa].reshape(NS, FB))
            x[a, blocks[f], rowsl(r), colsl(c)] = got.astype(BF16)
            if f == 0:
                y_copy(a, r, 0).start()
                y_copy(a, r, 1).start()
            core_copy(a, f, r).start()

    def forward(a, k):
        @pl.loop(0, n_chunks)
        def _(r):
            y_wait(a, r, 1 if k == 2 else 0)
            core_copy(a, k, r).start()

    def project(a, k):
        yy = blocks[k]
        rows = pl.ds(pl.multiple_of(yy * YB, YB), YB)
        if a == 0:
            wloads[k][0].wait()
            wloads[k][1].wait()
        else:
            wloads[k][2].wait()

        @pl.loop(0, n_chunks)
        def _(r):
            core_wait(a, k, r)
            left = x[a, yy, rowsl(r), :]
            for n in range(FH // 256):
                ns = pl.ds(n * 256, 256)
                if a == 0:
                    outs = ((0, nn(left, wg[rows, ns])), (1, nn(left, wu[rows, ns])))
                else:
                    outs = ((2, nt(left, wd[ns, rows])),)
                for i, v in outs:
                    if k == 0:
                        acc[i, rowsl(r), ns] = v
                    else:
                        acc[i, rowsl(r), ns] += v

    compact(0, 0)
    compact(0, 1)
    project(0, 0)
    compact(1, 0)
    compact(1, 1)
    project(1, 0)
    forward(0, 2)
    forward(0, 3)
    project(0, 1)
    project(1, 1)
    forward(1, 2)
    forward(1, 3)
    project(0, 2)
    project(0, 3)
    project(1, 2)
    project(1, 3)

    keep = jnp.concatenate(
        [jnp.broadcast_to(mask[:, j:j + 1].astype(F32), (1, 128)) for j in range(8)], axis=1)
    eye = iota((128, 128), 0) == iota((128, 128), 1)

    @pl.loop(0, n_chunks * 2)
    def _(i):
        rows = pl.ds(pl.multiple_of(i * 128, 128), 128)
        gate_in = acc[0, rows, :]
        up_in = acc[1, rows, :]
        back = acc[2, rows, :]
        sig = jax.nn.sigmoid(gate_in)
        swish = gate_in * sig
        slope = sig * (1.0 + gate_in * (1.0 - sig))
        act = (swish * up_in * keep).astype(BF16).astype(F32)
        score = jnp.sum(act * back, axis=1, keepdims=True)
        hidden = back * keep
        gd[rows, :] = (hidden * up_in * slope).astype(BF16)
        ud[rows, :] = (hidden * swish).astype(BF16)
        srecv[h, :, pl.ds(pl.multiple_of(i * 128, 128), 128)] = jnp.sum(
            jnp.where(eye, score, 0.0), axis=0, keepdims=True)

    def score_copy(k):
        to = lax.rem(h + k, 8)
        return remote(srecv.at[h], srecv.at[h], ss.at[to], rs.at[h], hidden=to)

    @pl.loop(1, 8)
    def _(k):
        score_copy(k).start()

    order = (1, 2, 3, 0)

    def terms(j):
        yy = blocks[order[j]]

        @pl.loop(0, n_chunks)
        def _(r):
            gdr = gd[rowsl(r), :]
            udr = ud[rowsl(r), :]
            for n in range(YB // 256):
                ws = pl.ds(pl.multiple_of(yy * YB + n * 256, 256), 256)
                acc[j % 3, rowsl(r), n * 256:(n + 1) * 256] = nt(gdr, wg[ws, :]) + nt(udr, wu[ws, :])
            stage[j, rowsl(r), :] = acc[j % 3, rowsl(r), colsl(oc)].astype(BF16)
            pair_copy(j, r).start()

    def pair_copy(j, r):
        return remote(stage.at[j, rowsl(r), :], crecv.at[j, rowsl(r), :], scc.at[j, r], rcc.at[j, r],
                      hidden=y * 2 + oc)

    def half_copy(r, way):
        rows = pl.ds(pl.multiple_of(r * RC + way * 128, 128), 128)
        land = (arecv, brecv)[way]
        return remote(fstage.at[rows, :], land.at[r], sab.at[r, way], rab.at[r, way],
                      hidden=(up, dn)[way] * 2 + c)

    def full_copy(r, way):
        return remote((ustage, dstage)[way].at[rowsl(r), :], (urecv, drecv)[way].at[rowsl(r), :],
                      sud.at[r, way], rud.at[r, way], hidden=(up, dn)[way] * 2 + c)

    def pair_sum(j, r):
        pair_copy(j, r).wait_recv()
        return acc[j % 3, rowsl(r), colsl(c)] + crecv[j, rowsl(r), :].astype(F32)

    def finish(j):
        @pl.loop(0, n_chunks)
        def _(r):
            v = pair_sum(j, r)
            if j == 0:
                fstage[rowsl(r), :] = v.astype(BF16)
                half_copy(r, 0).start()
                half_copy(r, 1).start()
            elif j in (1, 2):
                way = j - 1
                half_copy(r, way).wait_recv()
                extra = (arecv, brecv)[way][r].astype(F32)
                zero = jnp.zeros_like(extra)
                pieces = [extra, zero] if way == 0 else [zero, extra]
                v = v + jnp.concatenate(pieces, axis=0)
                (ustage, dstage)[way][rowsl(r), :] = v.astype(BF16)
                full_copy(r, way).start()
            else:
                full_copy(r, 0).wait_recv()
                full_copy(r, 1).wait_recv()
                v = v + urecv[rowsl(r), :].astype(F32) + drecv[rowsl(r), :].astype(F32)
                rgm[rowsl(r), :] = v.astype(BF16)

    terms(0)
    terms(1)
    finish(0)
    terms(2)
    finish(1)
    terms(3)
    finish(2)

    def slot_copy(d):
        return remote(scs.at[d], scr.at[me], sq.at[d], rq.at[me], expert=d)

    @pl.loop(1, 8)
    def _(k):
        frm = lax.rem(h + k, 8)
        remote(srecv.at[h], srecv.at[frm], ss.at[frm], rs.at[frm], hidden=frm).wait_recv()

    total = srecv[0]
    for k in range(1, 8):
        total = total + srecv[k]
    total = total.astype(BF16).astype(F32)
    for part in range(4):
        rows = pl.ds(part * (NS // 4), NS // 4)
        scol = jnp.sum(ptmat[rows, :].astype(F32) * total, axis=1, keepdims=True)
        put = jnp.where(iota((NS // 4, 128), 1) == kcol, scol, 0.0).astype(BF16)
        scs[pl.ds(part * 4, 4)] = put.reshape(4, SL, 128)

    @pl.loop(1, NE)
    def _(k):
        slot_copy(lax.rem(me + k, NE)).start()

    scr[me] = scs[me]

    finish(3)

    @pl.when(jnp.logical_not(is_text))
    def _():
        rgm[RC:, :] = jnp.zeros((TD - RC, FB), BF16)

    vsend[...] = nn(ptmat[...], rgm[...]).astype(BF16).reshape(NE, SL, FB)

    def row_copy(d, n):
        return remote(vsend.at[d, pl.ds(0, n), :], vrecv.at[me, pl.ds(0, n), :], sv.at[d], rv.at[me], expert=d)

    def row_wait(s, n):
        remote(vsend.at[s, pl.ds(0, n), :], vrecv.at[s, pl.ds(0, n), :], sv.at[s], rv.at[s], expert=s).wait_recv()

    @pl.when(is_text)
    def _():
        @pl.loop(1, NE)
        def _(k):
            row_copy(lax.rem(me + k, NE), SL).start()

    @pl.when(jnp.logical_not(is_text))
    def _():
        @pl.loop(1, NE)
        def _(k):
            row_copy(lax.rem(me + k, NE), 32).start()

    vrecv[me, :32, :] = vsend[me, :32, :]

    @pl.when(is_text)
    def _():
        vrecv[me, 32:, :] = vsend[me, 32:, :]

    @pl.loop(0, NE)
    def _(s):
        @pl.when(s != me)
        def _():
            remote(scs.at[s], scr.at[s], sq.at[s], rq.at[s], expert=s).wait_recv()

    rg[...] = nn(omat[...], scr[...].reshape(NS, 128))[:, :EH].astype(BF16)

    @pl.loop(0, EH)
    def _(s):
        @pl.when(s != me)
        def _():
            row_wait(s, SL)

    @pl.loop(EH, NE)
    def _(s):
        @pl.when(s != me)
        def _():
            row_wait(s, 32)

    ig[...] = nn(gmat[...], vrecv[...].reshape(NS, FB)).astype(BF16)

    for f in range(2):
        @pl.loop(0, EH)
        def _(d):
            @pl.when(d != me)
            def _():
                text_copy(f, 0, d).wait_send()
                text_copy(f, 1, d).wait_send()

            @pl.when(EH + d != me)
            def _():
                image_copy(f, d).wait_send()

    @pl.loop(0, n_chunks)
    def _(r):
        for a in range(2):
            y_copy(a, r, 0).wait_send()
            y_copy(a, r, 1).wait_send()
            for k in range(4):
                core_copy(a, k, r).wait_send()
        for j in range(4):
            pair_copy(j, r).wait_send()
        for way in range(2):
            half_copy(r, way).wait_send()
            full_copy(r, way).wait_send()

    @pl.loop(1, 8)
    def _(k):
        score_copy(k).wait_send()

    @pl.loop(1, NE)
    def _(k):
        slot_copy(lax.rem(me + k, NE)).wait_send()

    @pl.when(is_text)
    def _():
        @pl.loop(1, NE)
        def _(k):
            row_copy(lax.rem(me + k, NE), SL).wait_send()

    @pl.when(jnp.logical_not(is_text))
    def _():
        @pl.loop(1, NE)
        def _(k):
            row_copy(lax.rem(me + k, NE), 32).wait_send()


def body(tokens, out_grad, gates, labels, text_picks, image_picks, block_mask, w_gate, w_up, w_down):
    any_spec = pl.BlockSpec(memory_space=pl.ANY)
    vmem = pl.BlockSpec(memory_space=pltpu.VMEM)
    dma = pltpu.SemaphoreType.DMA
    return pl.pallas_call(
        kernel,
        out_shape=(
            jax.ShapeDtypeStruct((TD, FB), BF16),
            jax.ShapeDtypeStruct((TD, EH), BF16),
        ),
        in_specs=[any_spec, any_spec, vmem, vmem, vmem, vmem, vmem, any_spec, any_spec, any_spec],
        out_specs=(vmem, vmem),
        scratch_shapes=[
            pltpu.VMEM((D, FH), BF16),
            pltpu.VMEM((D, FH), BF16),
            pltpu.VMEM((FH, D), BF16),
            pltpu.VMEM((2, 2 * TD, FB), BF16),
            pltpu.VMEM((TD, TD), BF16),
            pltpu.VMEM((TD, TD), BF16),
            pltpu.VMEM((NE, HALF), F32),
            pltpu.VMEM((EH * SL, TD), BF16),
            pltpu.VMEM((EH * SL, 2 * TD), BF16),
            pltpu.VMEM((TD, NS), BF16),
            pltpu.VMEM((TD, NS), BF16),
            pltpu.VMEM((2, TD, NS), BF16),
            pltpu.VMEM((NS, TD), BF16),
            pltpu.VMEM((2, 2, EH, SL, FB), BF16),
            pltpu.VMEM((2, EH, SL, FB), BF16),
            pltpu.VMEM((2, 2, NE, SL, FB), BF16),
            pltpu.VMEM((2, 4, TD, YB), BF16),
            pltpu.VMEM((3, TD, FH), F32),
            pltpu.VMEM((TD, FH), BF16),
            pltpu.VMEM((TD, FH), BF16),
            pltpu.VMEM((4, TD, FB), BF16),
            pltpu.VMEM((4, TD, FB), BF16),
            pltpu.VMEM((TD, FB), BF16),
            pltpu.VMEM((TD, FB), BF16),
            pltpu.VMEM((TD, FB), BF16),
            pltpu.VMEM((2, 128, FB), BF16),
            pltpu.VMEM((2, 128, FB), BF16),
            pltpu.VMEM((TD, FB), BF16),
            pltpu.VMEM((TD, FB), BF16),
            pltpu.VMEM((TD, FB), BF16),
            pltpu.VMEM((NE, SL, FB), BF16),
            pltpu.VMEM((NE, SL, FB), BF16),
            pltpu.VMEM((8, 1, TD), F32),
            pltpu.VMEM((NE, SL, 128), BF16),
            pltpu.VMEM((NE, SL, 128), BF16),
            dma((2, 2)),
            dma((4, 3)),
            dma((2, 2, EH)),
            dma((2, EH)),
            dma((2, 2, NE)),
            dma((2, 2, 2)),
            dma((2, 2, 2)),
            dma((2, 4, 2)),
            dma((2, 4, 2)),
            dma((8,)),
            dma((8,)),
            dma((4, 2)),
            dma((4, 2)),
            dma((2, 2)),
            dma((2, 2)),
            dma((2, 2)),
            dma((2, 2)),
            dma((NE,)),
            dma((NE,)),
            dma((NE,)),
            dma((NE,)),
        ],
        compiler_params=pltpu.CompilerParams(
            collective_id=0, has_side_effects=True, vmem_limit_bytes=62 * 1024 * 1024),
        cost_estimate=pl.CostEstimate(flops=16_000_000_000, bytes_accessed=22_000_000, transcendentals=1_000_000),
    )(
        tokens, out_grad, gates, labels.reshape(1, TD), text_picks, image_picks, block_mask,
        w_gate[0], w_up[0], w_down[0],
    )


def solution(mesh):
    placed = (
        P("expert", None),
        P("expert", None),
        P("expert", None),
        P("expert"),
        P(),
        P(),
        P("expert", "hidden"),
        P("expert", None, "hidden"),
        P("expert", None, "hidden"),
        P("expert", "hidden", None),
    )
    return jax.shard_map(
        body,
        mesh=mesh,
        in_specs=placed,
        out_specs=(P("expert", "hidden"), P("expert", None)),
        check_vma=False,
    )
```

time: 455 us -> 93.3 us (0.21)
  local copies, waits for them, and re-layouts: 155 us -> 4.85 us
  blocking collectives: 133 us -> 0 us
  Pallas kernels: 0 us -> 87.5 us
  waiting for transfers between devices: 61.4 us -> 0 us
  matrix products: 51.9 us -> 0 us
  other arithmetic: 21 us -> 0 us
  starting transfers between devices: 16.8 us -> 0 us
  between operations: 14.4 us -> 0.64 us
    all_to_all x2 -> x0, blocking collectives: 120 us -> none  [the longest x1 63.2 us: body(): lax.all_to_all(pick_rows(tokens), 'expert', split_axis=0, concat_axis=0,...]
    pallas_call x0 -> x1, Pallas kernels: none -> 87.5 us  [body(): pl.pallas_call(kernel, out_shape=(jax.ShapeDtypeStruct((TD, FB), BF16), j...]
    unnamed x28 -> x2, local copies, waits for them, and re-layouts: 89.8 us -> 3.27 us
    gather x6 -> x0, local copies, waits for them, and re-layouts: 62.6 us -> none  [the longest x2 39.1 us: place_slots(): local_rows = token_order[offset + pick_ranks % half_count]]
    dot_general x7 -> x0, matrix products: 51.9 us -> none  [the longest x3 31.5 us: contract_last(): lax.dot_general(left_rows, right_rows, (((1,), (1,)), ((), ())), preferre...]
    all_to_all x3 -> x0, waiting for transfers between devices: 50.2 us -> none  [the longest x1 42.9 us: body(): lax.all_to_all(pick_rows(out_grad), 'expert', split_axis=0, concat_axis=0...]
    all_to_all x3 -> x0, starting transfers between devices: 16.5 us -> none  [the longest x1 7.96 us: body(): lax.all_to_all(gate_send, 'expert', split_axis=0, concat_axis=0, tiled=True)]
    psum x1 -> x0, blocking collectives: 12.5 us -> none  [body(): score_total = lax.psum(local_score, 'hidden')]
  transfers between devices with their start and end apart: 4 -> 0, of which waited for: 3 -> 0; matrix products, arithmetic and copies ran while one was open for 10% -> 0% of each run, Pallas kernels for 0% -> 0%
where the time goes in v1:
time: 93.3 us; the launch traced here: 93 us
  Pallas kernels  87.5 us (94%)
  local copies, waits for them, and re-layouts  4.85 us (5%)
    pallas_call x1, Pallas kernels, body(): pl.pallas_call(kernel, out_shape=(jax.ShapeDtypeStruct((TD, FB), BF16), j...  87.5 us
    unnamed x2, local copies, waits for them, and re-layouts  3.27 us

profile of v1, /device:TPU:0, one launch (start us, length us, event | category | flops | bytes accessed | tf_op | source)
XLA Modules:
  0.0 93.0 jit_solution(7906748549941721539)
XLA Ops:
  0.6 1.5 %copy.12.gates = bf16[512,8]{1,0:T(8,128)(2,1)} copy(bf16[512,8]{0,1:T(8,128)(2,1)} %param.12) | data formatting | bytes 16384 | tf_op args[2]
  2.1 87.5 %shard_map.113 = (bf16[512,384]{1,0:T(8,128)(2,1)}, bf16[512,8]{1,0:T(8,128)(2,1)}) custom-call(bf16[512,3072]{1,0:T(8,128)(2,1)} %tok_h.1, bf16[512,3072]{1,0:T(8,128)(2,1)} %og_h.1, bf16[512,8]{1,0:T(8,128)(2,1)} %copy.12.gates, s32[1,512]{1,0:T(1,128)} %bitcast.7, s32[8,512]{1,0:T(8,128)} %tpk.1, s32[8,256]{1,0:T(8,128)} %ipk.1, s32[1,8]{1,0:T(1,128)} %mask.1, ...), custom_call_target="tpu_custom_call" | custom-call | flops 16000000000 | bytes 22000000 | tf_op jit(solution)/shard_map/pallas_call | solution.py:532
  89.7 1.6 %copy.13 = bf16[512,8]{0,1:T(8,128)(2,1)} copy(bf16[512,8]{1,0:T(8,128)(2,1)} %get-tuple-element.3) | data formatting | bytes 16384 | tf_op jit(solution)/shard_map/pallas_call | solution.py:532
  91.2 1.8 %copy.15 = bf16[512,384]{1,0:T(8,128)(2,1)} copy(bf16[512,384]{1,0:T(8,128)(2,1)} %get-tuple-element.6) | data formatting | bytes 786432

commit v2 on v1

v2 whole, which is shorter than its diff:
```python
import jax
import jax.numpy as jnp
from jax import lax
from jax.experimental import pallas as pl
from jax.experimental.pallas import tpu as pltpu
from jax.sharding import PartitionSpec as P

MESH = pl.DeviceIdType.MESH
F32 = jnp.float32
BF16 = jnp.bfloat16

TD = 512
HALF = 256
NE = 16
EH = 8
SL = 48
SI = 24
NS = NE * SL
D = 3072
FB = 384
YB = 768
FH = 1024
RC = 256
PART = (0, 256, 384)


def nt(a, b):
    return lax.dot_general(a, b, (((1,), (1,)), ((), ())), preferred_element_type=F32)


def nn(a, b):
    return jnp.dot(a, b, preferred_element_type=F32)


def iota(shape, dim):
    return lax.broadcasted_iota(jnp.int32, shape, dim)


def one(cond):
    return jnp.where(cond, 1.0, 0.0).astype(F32)


def kernel(
    tok_h, og_h, gates, labels, tpk, ipk, mask, wg_h, wu_h, wd_h,
    ig, rg,
    wg, wu, wd, cols, tri, idn, mref, smat, s2mat, gmat, omat, pmat, ptmat,
    send_t, send_i, recv, x, acc, gd, ud, stage, crecv, fstage, ustage, dstage,
    arecv, brecv, urecv, drecv, rgm, vsend, vrecv, ssend, sland, srecv,
    ld_sem, w_sem, s1t, s1i, r1, sy, ry, sc, rc, ss, rs, scc, rcc, sab, rab, sud, rud,
    sv, rv,
):
    me = lax.axis_index("expert")
    h = lax.axis_index("hidden")
    y = lax.div(h, 2)
    c = lax.rem(h, 2)
    oc = 1 - c
    far = lax.rem(y + 2, 4)
    up = lax.rem(y + 1, 4)
    dn = lax.rem(y + 3, 4)
    kcol = lax.rem(me, EH)
    is_text = me < EH
    n_chunks = 2 - lax.div(me, EH)
    blocks = (y, far, up, dn)

    def remote(src, dst, s_sem, r_sem, **where):
        return pltpu.make_async_remote_copy(
            src_ref=src, dst_ref=dst, send_sem=s_sem, recv_sem=r_sem,
            device_id=where, device_id_type=MESH,
        )

    def colsl(core):
        return pl.ds(pl.multiple_of(core * FB, 128), FB)

    def rowsl(r):
        return pl.ds(pl.multiple_of(r * RC, RC), RC)

    leave = []
    text_gone = {}

    def both(rows_of):
        @pl.when(is_text)
        def _():
            rows_of(TD)

        @pl.when(jnp.logical_not(is_text))
        def _():
            rows_of(RC)

    loads = []
    for f, yy in enumerate((y, far)):
        fs = pl.ds(pl.multiple_of((yy * 2 + c) * FB, 128), FB)
        for a, src in enumerate((tok_h, og_h)):
            cp = pltpu.make_async_copy(
                src.at[:, fs], cols.at[f, pl.ds(a * TD, TD), :], ld_sem.at[f, a])
            cp.start()
            loads.append(cp)
    wloads = []
    for k, yy in enumerate(blocks):
        rows = pl.ds(pl.multiple_of(yy * YB, YB), YB)
        trio = [
            pltpu.make_async_copy(wg_h.at[rows, :], wg.at[rows, :], w_sem.at[k, 0]),
            pltpu.make_async_copy(wu_h.at[rows, :], wu.at[rows, :], w_sem.at[k, 1]),
            pltpu.make_async_copy(wd_h.at[:, rows], wd.at[:, rows], w_sem.at[k, 2]),
        ]
        for cp in trio:
            cp.start()
        wloads.append(trio)

    barrier = pltpu.get_barrier_semaphore()

    @pl.loop(1, NE)
    def _(k):
        pl.semaphore_signal(barrier, inc=1, device_id={"expert": lax.rem(me + k, NE)}, device_id_type=MESH)

    @pl.loop(1, 8)
    def _(k):
        pl.semaphore_signal(barrier, inc=1, device_id={"hidden": lax.rem(h + k, 8)}, device_id_type=MESH)

    r5 = iota((TD, TD), 0)
    c5 = iota((TD, TD), 1)
    tri[...] = one(r5 <= c5).astype(BF16)
    idn[...] = one(r5 == c5).astype(BF16)
    text = one(labels[...] == 0)
    lab16 = jnp.where(iota((NE, TD), 0) < EH, text, 1.0 - text)
    rank = nn(lab16.astype(BF16), tri[...])
    key = jnp.where(lab16 > 0.0, rank - 1.0, -1.0)

    def local_rank(p):
        return jnp.where(lax.shift_right_logical(p, 8) == me, (p & 255), -1).astype(F32)

    lov = jnp.concatenate([
        local_rank(tpk[...]),
        jnp.concatenate([local_rank(ipk[...]), jnp.full((EH, TD - HALF), -1.0, F32)], axis=1),
    ], axis=0)
    lov_t = nt(idn[...], lov.astype(BF16))
    rrow = iota((1, HALF), 1).astype(F32)
    def slots(e0, depth):
        for e in range(e0, e0 + EH):
            hit = one(lov_t[:depth, e:e + 1] == rrow)
            mref[e:e + 1, :] = jnp.sum(hit, axis=0, keepdims=True)
        member = mref[e0:e0 + EH, :]
        slot = member * nn(member.astype(BF16), tri[:HALF, :HALF])
        rcol = iota((HALF, TD), 0).astype(F32)
        return nn(slot.astype(BF16), one(rcol == key[e0:e0 + 1, :]).astype(BF16))

    st_text = slots(0, TD)
    s1 = iota((SL, TD), 0).astype(F32) + 1.0
    for e in range(EH):
        smat[e * SL:(e + 1) * SL, :] = one(st_text[e:e + 1, :] == s1).astype(BF16)

    pl.semaphore_wait(barrier, NE - 1 + 7)

    def text_copy(f, a, d):
        return remote(send_t.at[f, a, d], recv.at[f, a, me], s1t.at[f, a, d], r1.at[f, a, me], expert=d)

    def image_copy(f, d):
        return remote(send_i.at[f, d], recv.at[f, 0, me], s1i.at[f, d], r1.at[f, 0, me], expert=EH + d)

    def pick_text(f, a):
        loads[f * 2 + a].wait()
        t = nn(smat[...], cols[f, a * TD:(a + 1) * TD, :])
        send_t[f, a] = t.astype(BF16).reshape(EH, SL, FB)

        @pl.loop(0, EH)
        def _(k):
            d = lax.rem(me + k, EH)

            @pl.when(d != me)
            def _():
                text_copy(f, a, d).start()

            @pl.when(d == me)
            def _():
                recv[f, a, me] = send_t[f, a, d]

        def gone():
            @pl.loop(0, EH)
            def _(d):
                @pl.when(d != me)
                def _():
                    text_copy(f, a, d).wait_send()

        text_gone[f, a] = gone

    def left(f, a):
        text_gone.pop((f, a))()

    def pick_image(f):
        t = nn(s2mat[...], cols[f])
        send_i[f] = t.astype(BF16).reshape(EH, SL, FB)

        @pl.loop(0, EH)
        def _(k):
            d = lax.rem(me + k, EH)

            @pl.when(EH + d != me)
            def _():
                image_copy(f, d).start()

            @pl.when(EH + d == me)
            def _():
                recv[f, 0, me] = send_i[f, d]

        @leave.append
        def _():
            @pl.loop(0, EH)
            def _(d):
                @pl.when(EH + d != me)
                def _():
                    image_copy(f, d).wait_send()

    pick_text(0, 0)

    st_image = slots(EH, HALF)
    for e in range(EH):
        im = st_image[e:e + 1, :]
        s2mat[e * SL:(e + 1) * SL, :TD] = one(im == s1).astype(BF16)
        im2 = jnp.where(im > 0.0, im + SI, -1.0)
        s2mat[e * SL:(e + 1) * SL, TD:] = one(im2 == s1).astype(BF16)

    jq_row = jnp.floor((iota((1, NS), 1).astype(F32) + 0.5) * (1.0 / SL))
    jr_row = iota((1, NS), 1).astype(F32) - jq_row * SL
    jq_col = jnp.floor((iota((NS, 1), 0).astype(F32) + 0.5) * (1.0 / SL))
    jr_col = iota((NS, 1), 0).astype(F32) - jq_col * SL

    def source(p):
        return lax.shift_right_logical(p, 8).astype(F32)

    src_text = source(tpk[pl.ds(kcol, 1), :])
    src_image = jnp.concatenate(
        [source(ipk[pl.ds(kcol, 1), :]), jnp.full((1, TD - HALF), 99.0, F32)], axis=1)
    src = jnp.where(is_text, src_text, src_image)
    i16 = iota((NE, 1), 0).astype(F32)
    cnt16 = jnp.sum(one(src == i16), axis=1, keepdims=True)
    off16 = jnp.sum(one(src < i16), axis=1, keepdims=True)
    spread = iota((NE, NS), 0).astype(F32) == jq_row
    cnt_row = jnp.sum(jnp.where(spread, cnt16, 0.0), axis=0, keepdims=True)
    off_row = jnp.sum(jnp.where(spread, off16, 0.0), axis=0, keepdims=True)
    for a in range(2):
        shift = (lax.div(me, EH) * (SI * a)).astype(F32)
        place = jr_row - shift
        good = jnp.where((place >= 0.0) & (place < cnt_row), off_row + place, -1.0)
        pmat[a] = one(iota((TD, NS), 0).astype(F32) == good).astype(BF16)
    cnt_col = jnp.sum(one(src == jq_col), axis=1, keepdims=True)
    off_col = jnp.sum(one(src < jq_col), axis=1, keepdims=True)
    good_col = jnp.where(jr_col < cnt_col, off_col + jr_col, -1.0)
    ptmat[...] = one(iota((NS, TD), 1).astype(F32) == good_col).astype(BF16)

    def owner_tables():
        st = jnp.concatenate([st_text, st_image], axis=0)
        st_t = nt(idn[...], st.astype(BF16)).astype(BF16)
        st_wide = nn(st_t, one(spread).astype(BF16))
        filled = st_wide == jr_row + 1.0
        omat[...] = one(filled).astype(BF16)
        k_row = jnp.where(jq_row >= EH, jq_row - EH, jq_row)
        spread_k = one(iota((EH, NS), 0).astype(F32) == k_row).astype(BF16)
        gate_wide = nn(nt(idn[...], gates[...]).astype(BF16), spread_k)
        gmat[...] = jnp.where(filled, gate_wide, 0.0).astype(BF16)

    vrecv[EH:, 32:, :] = jnp.zeros((EH, SL - 32, FB), BF16)
    sland[EH:, 32:, :] = jnp.zeros((EH, SL - 32, 128), BF16)

    @pl.when(jnp.logical_not(is_text))
    def _():
        rgm[RC:, :] = jnp.zeros((TD - RC, FB), BF16)

    srecv[h] = jnp.zeros((1, TD), F32)

    def y_copy(a, r, way):
        ref = x.at[a, y, rowsl(r), colsl(c)]
        return remote(ref, ref, sy.at[a, r, way], ry.at[a, r, way], hidden=(up, dn)[way] * 2 + c)

    def y_wait(a, r, way):
        ref = x.at[a, (dn, up)[way], rowsl(r), colsl(c)]
        remote(ref, ref, sy.at[a, r, way], ry.at[a, r, way], hidden=(dn, up)[way] * 2 + c).wait_recv()

    def core_copy(a, k, r):
        ref = x.at[a, blocks[k], rowsl(r), colsl(c)]
        return remote(ref, ref, sc.at[a, k, r], rc.at[a, k, r], hidden=y * 2 + oc)

    def core_wait(a, k, r):
        ref = x.at[a, blocks[k], rowsl(r), colsl(oc)]
        remote(ref, ref, sc.at[a, k, r], rc.at[a, k, r], hidden=y * 2 + oc).wait_recv()

    def chunks_left(*copies, only=None):
        def wait():
            @pl.loop(0, n_chunks)
            def _(r):
                for copy in copies:
                    copy(r).wait_send()

        leave.append(wait if only is None else lambda: pl.when(only)(wait))

    def compact(f, a, text_expert):
        aa = a if text_expert else 0

        @pl.when(is_text if text_expert else jnp.logical_not(is_text))
        def _():
            if text_expert or a == 0:
                @pl.loop(0, NE)
                def _(s):
                    @pl.when(s != me)
                    def _():
                        remote(send_t.at[f, a, 0], recv.at[f, aa, s], s1t.at[f, a, 0], r1.at[f, aa, s],
                               expert=s).wait_recv()

            @pl.loop(0, 2 if text_expert else 1)
            def _(r):
                got = nn(pmat[a, rowsl(r), :], recv[f, aa].reshape(NS, FB))
                x[a, blocks[f], rowsl(r), colsl(c)] = got.astype(BF16)
                if f == 0:
                    y_copy(a, r, 0).start()
                    y_copy(a, r, 1).start()
                core_copy(a, f, r).start()

        copies = [lambda r: core_copy(a, f, r)]
        if f == 0:
            copies += [lambda r: y_copy(a, r, 0), lambda r: y_copy(a, r, 1)]
        chunks_left(*copies, only=is_text if text_expert else jnp.logical_not(is_text))

    def forward(a, k):
        @pl.loop(0, n_chunks)
        def _(r):
            y_wait(a, r, 1 if k == 2 else 0)
            core_copy(a, k, r).start()

        chunks_left(lambda r: core_copy(a, k, r))

    def project(a, k):
        yy = blocks[k]
        rows = pl.ds(pl.multiple_of(yy * YB, YB), YB)
        if a == 0:
            wloads[k][0].wait()
            wloads[k][1].wait()
        else:
            wloads[k][2].wait()

        @pl.loop(0, n_chunks)
        def _(r):
            core_wait(a, k, r)

        def rows_of(m):
            left = x[a, yy, :m, :]
            for n in range(FH // 256):
                ns = pl.ds(n * 256, 256)
                if a == 0:
                    outs = ((0, nn(left, wg[rows, ns])), (1, nn(left, wu[rows, ns])))
                else:
                    outs = ((2, nt(left, wd[ns, rows])),)
                for i, v in outs:
                    if k == 0:
                        acc[i, :m, ns] = v
                    else:
                        acc[i, :m, ns] += v

        both(rows_of)

    pick_text(0, 1)
    pick_image(0)
    left(0, 0)
    pick_text(1, 0)
    compact(0, 0, True)
    left(0, 1)
    pick_text(1, 1)
    pick_image(1)
    compact(0, 1, True)
    compact(0, 0, False)
    compact(0, 1, False)
    owner_tables()
    project(0, 0)
    forward(0, 2)
    forward(0, 3)
    compact(1, 0, True)
    project(1, 0)
    project(0, 2)
    project(0, 3)
    compact(1, 0, False)
    compact(1, 1, False)
    compact(1, 1, True)
    project(0, 1)
    forward(1, 2)
    forward(1, 3)
    project(1, 1)
    project(1, 2)
    project(1, 3)

    keep = jnp.concatenate(
        [jnp.broadcast_to(mask[:, j:j + 1].astype(F32), (1, 128)) for j in range(8)], axis=1)
    eye = iota((128, 128), 0) == iota((128, 128), 1)

    @pl.loop(0, n_chunks * 2)
    def _(i):
        rows = pl.ds(pl.multiple_of(i * 128, 128), 128)
        gate_in = acc[0, rows, :]
        up_in = acc[1, rows, :]
        back = acc[2, rows, :]
        sig = jax.nn.sigmoid(gate_in)
        swish = gate_in * sig
        slope = sig * (1.0 + gate_in * (1.0 - sig))
        act = (swish * up_in * keep).astype(BF16).astype(F32)
        score = jnp.sum(act * back, axis=1, keepdims=True)
        hidden = back * keep
        gd[rows, :] = (hidden * up_in * slope).astype(BF16)
        ud[rows, :] = (hidden * swish).astype(BF16)
        srecv[h, :, pl.ds(pl.multiple_of(i * 128, 128), 128)] = jnp.sum(
            jnp.where(eye, score, 0.0), axis=0, keepdims=True)

    def score_copy(k):
        to = lax.rem(h + k, 8)
        return remote(srecv.at[h], srecv.at[h], ss.at[to], rs.at[h], hidden=to)

    @pl.loop(1, 8)
    def _(k):
        score_copy(k).start()

    @leave.append
    def _():
        @pl.loop(1, 8)
        def _(k):
            score_copy(k).wait_send()

    order = (1, 2, 3, 0)

    def part(s):
        return slice(PART[s], PART[s + 1])

    def kept(s, j):
        return j // 2, slice(j % 2 * FB + PART[s], j % 2 * FB + PART[s + 1])

    def pair_copy(s, j, n):
        ref = stage.at[j, pl.ds(0, n), part(s)], crecv.at[j, pl.ds(0, n), part(s)]
        return remote(*ref, scc.at[s, j], rcc.at[s, j], hidden=y * 2 + oc)

    def half(way, n):
        return pl.ds(way * (n // 2), n // 2)

    def half_copy(s, way, n):
        land = (arecv, brecv)[way]
        return remote(fstage.at[half(way, n), part(s)], land.at[pl.ds(0, n // 2), part(s)],
                      sab.at[s, way], rab.at[s, way], hidden=(up, dn)[way] * 2 + c)

    def full_copy(s, way, m, n):
        return remote((ustage, dstage)[way].at[half(m, n), part(s)], (urecv, drecv)[way].at[half(m, n), part(s)],
                      sud.at[s, way, m], rud.at[s, way, m], hidden=(up, dn)[way] * 2 + c)

    def later(copy):
        leave.append(lambda: both(lambda n: copy(n).wait_send()))

    def terms(s, j):
        wide = PART[s + 1] - PART[s]
        base = blocks[order[j]] * YB + PART[s]
        mine = pl.ds(pl.multiple_of(base + c * FB, 128), wide)
        other = pl.ds(pl.multiple_of(base + oc * FB, 128), wide)
        at, lanes = kept(s, j)

        def rows_of(n):
            wgs = jnp.concatenate([wg[mine, :], wg[other, :]], axis=0)
            wus = jnp.concatenate([wu[mine, :], wu[other, :]], axis=0)
            v = nt(gd[:n, :], wgs) + nt(ud[:n, :], wus)
            stage[j, :n, part(s)] = v[:, wide:].astype(BF16)
            pair_copy(s, j, n).start()
            acc[at, :n, lanes] = v[:, :wide]

        both(rows_of)
        later(lambda n: pair_copy(s, j, n))

    def pair_sum(s, j, m, n):
        at, lanes = kept(s, j)
        return acc[at, half(m, n), lanes] + crecv[j, half(m, n), part(s)].astype(F32)

    def finish_far(s):
        def rows_of(n):
            pair_copy(s, 0, n).wait_recv()
            for way in range(2):
                fstage[half(way, n), part(s)] = pair_sum(s, 0, way, n).astype(BF16)
                half_copy(s, way, n).start()

        both(rows_of)
        later(lambda n: half_copy(s, 0, n))
        later(lambda n: half_copy(s, 1, n))

    def finish_free(s, way):
        def rows_of(n):
            pair_copy(s, 1 + way, n).wait_recv()
            (ustage, dstage)[way][half(1 - way, n), part(s)] = pair_sum(s, 1 + way, 1 - way, n).astype(BF16)
            full_copy(s, way, 1 - way, n).start()

        both(rows_of)
        later(lambda n: full_copy(s, way, 1 - way, n))

    def finish_rest(s, way):
        def rows_of(n):
            half_copy(s, way, n).wait_recv()
            v = pair_sum(s, 1 + way, way, n) + (arecv, brecv)[way][:n // 2, part(s)].astype(F32)
            (ustage, dstage)[way][half(way, n), part(s)] = v.astype(BF16)
            full_copy(s, way, way, n).start()

        both(rows_of)
        later(lambda n: full_copy(s, way, way, n))

    def finish_own(s):
        def rows_of(n):
            pair_copy(s, 3, n).wait_recv()
            for m in (1, 0):
                full_copy(s, 0, m, n).wait_recv()
                full_copy(s, 1, m, n).wait_recv()
                v = pair_sum(s, 3, m, n)
                v = v + urecv[half(m, n), part(s)].astype(F32) + drecv[half(m, n), part(s)].astype(F32)
                rgm[half(m, n), part(s)] = v.astype(BF16)

        both(rows_of)

    def row_copy(p, d, n):
        if p == len(PART) - 1:
            src, dst = ssend.at[d, pl.ds(0, n), :], sland.at[me, pl.ds(0, n), :]
        else:
            src, dst = vsend.at[d, pl.ds(0, n), part(p)], vrecv.at[me, pl.ds(0, n), part(p)]
        return remote(src, dst, sv.at[p, d], rv.at[p, me], expert=d)

    def row_wait(p, n, first, last):
        @pl.loop(first, last)
        def _(s):
            @pl.when(s != me)
            def _():
                if p == len(PART) - 1:
                    src, dst = ssend.at[s, pl.ds(0, n), :], sland.at[s, pl.ds(0, n), :]
                else:
                    src, dst = vsend.at[s, pl.ds(0, n), part(p)], vrecv.at[s, pl.ds(0, n), part(p)]
                remote(src, dst, sv.at[p, s], rv.at[p, s], expert=s).wait_recv()

    def row_send(p):
        def all_rows(act):
            @pl.when(is_text)
            def _():
                @pl.loop(1, NE)
                def _(k):
                    act(row_copy(p, lax.rem(me + k, NE), SL))

            @pl.when(jnp.logical_not(is_text))
            def _():
                @pl.loop(1, NE)
                def _(k):
                    act(row_copy(p, lax.rem(me + k, NE), 32))

        all_rows(lambda copy: copy.start())
        src, dst, lanes = (ssend, sland, slice(None)) if p == len(PART) - 1 else (vsend, vrecv, part(p))
        dst[me, :32, lanes] = src[me, :32, lanes]

        @pl.when(is_text)
        def _():
            dst[me, 32:, lanes] = src[me, 32:, lanes]

        leave.append(lambda: all_rows(lambda copy: copy.wait_send()))

    def send_scores():
        @pl.loop(1, 8)
        def _(k):
            frm = lax.rem(h + k, 8)
            remote(srecv.at[h], srecv.at[frm], ss.at[frm], rs.at[frm], hidden=frm).wait_recv()

        total = srecv[0]
        for k in range(1, 8):
            total = total + srecv[k]
        total = total.astype(BF16).astype(F32)
        for q in range(4):
            rows = pl.ds(q * (NS // 4), NS // 4)
            scol = jnp.sum(ptmat[rows, :].astype(F32) * total, axis=1, keepdims=True)
            put = jnp.where(iota((NS // 4, 128), 1) == kcol, scol, 0.0).astype(BF16)
            ssend[pl.ds(q * 4, 4)] = put.reshape(4, SL, 128)
        row_send(len(PART) - 1)

    def send_rows(s):
        finish_own(s)
        wide = PART[s + 1] - PART[s]
        vsend[:, :, part(s)] = nn(ptmat[...], rgm[:, part(s)]).astype(BF16).reshape(NE, SL, wide)
        row_send(s)

    def scores_here():
        row_wait(len(PART) - 1, SL, 0, EH)
        row_wait(len(PART) - 1, 32, EH, NE)
        rg[...] = jnp.transpose(nn(omat[...], sland[...].reshape(NS, 128)))[:EH].astype(BF16)

    def rows_here(s):
        row_wait(s, SL, 0, EH)
        row_wait(s, 32, EH, NE)
        wide = PART[s + 1] - PART[s]
        ig[:, part(s)] = nn(gmat[...], vrecv[:, :, part(s)].reshape(NS, wide)).astype(BF16)

    def flush():
        for wait in leave + list(text_gone.values()):
            wait()
        leave.clear()
        text_gone.clear()

    terms(0, 0)
    terms(0, 1)
    finish_far(0)
    terms(0, 2)
    finish_free(0, 0)
    terms(0, 3)
    finish_free(0, 1)
    terms(1, 0)
    finish_rest(0, 0)
    finish_rest(0, 1)
    terms(1, 1)
    finish_far(1)
    terms(1, 2)
    finish_free(1, 0)
    terms(1, 3)
    finish_free(1, 1)
    send_scores()
    finish_rest(1, 0)
    finish_rest(1, 1)
    send_rows(0)
    flush()
    send_rows(1)
    scores_here()
    rows_here(0)
    rows_here(1)

    flush()


def body(tokens, out_grad, gates, labels, text_picks, image_picks, block_mask, w_gate, w_up, w_down):
    any_spec = pl.BlockSpec(memory_space=pl.ANY)
    vmem = pl.BlockSpec(memory_space=pltpu.VMEM)
    dma = pltpu.SemaphoreType.DMA
    input_grad, router_grad = pl.pallas_call(
        kernel,
        out_shape=(
            jax.ShapeDtypeStruct((TD, FB), BF16),
            jax.ShapeDtypeStruct((EH, TD), BF16),
        ),
        in_specs=[any_spec, any_spec, vmem, vmem, vmem, vmem, vmem, any_spec, any_spec, any_spec],
        out_specs=(vmem, vmem),
        scratch_shapes=[
            pltpu.VMEM((D, FH), BF16),
            pltpu.VMEM((D, FH), BF16),
            pltpu.VMEM((FH, D), BF16),
            pltpu.VMEM((2, 2 * TD, FB), BF16),
            pltpu.VMEM((TD, TD), BF16),
            pltpu.VMEM((TD, TD), BF16),
            pltpu.VMEM((NE, HALF), F32),
            pltpu.VMEM((EH * SL, TD), BF16),
            pltpu.VMEM((EH * SL, 2 * TD), BF16),
            pltpu.VMEM((TD, NS), BF16),
            pltpu.VMEM((TD, NS), BF16),
            pltpu.VMEM((2, TD, NS), BF16),
            pltpu.VMEM((NS, TD), BF16),
            pltpu.VMEM((2, 2, EH, SL, FB), BF16),
            pltpu.VMEM((2, EH, SL, FB), BF16),
            pltpu.VMEM((2, 2, NE, SL, FB), BF16),
            pltpu.VMEM((2, 4, TD, YB), BF16),
            pltpu.VMEM((3, TD, FH), F32),
            pltpu.VMEM((TD, FH), BF16),
            pltpu.VMEM((TD, FH), BF16),
            pltpu.VMEM((4, TD, FB), BF16),
            pltpu.VMEM((4, TD, FB), BF16),
            pltpu.VMEM((TD, FB), BF16),
            pltpu.VMEM((TD, FB), BF16),
            pltpu.VMEM((TD, FB), BF16),
            pltpu.VMEM((TD // 2, FB), BF16),
            pltpu.VMEM((TD // 2, FB), BF16),
            pltpu.VMEM((TD, FB), BF16),
            pltpu.VMEM((TD, FB), BF16),
            pltpu.VMEM((TD, FB), BF16),
            pltpu.VMEM((NE, SL, FB), BF16),
            pltpu.VMEM((NE, SL, FB), BF16),
            pltpu.VMEM((NE, SL, 128), BF16),
            pltpu.VMEM((NE, SL, 128), BF16),
            pltpu.VMEM((8, 1, TD), F32),
            dma((2, 2)),
            dma((4, 3)),
            dma((2, 2, EH)),
            dma((2, EH)),
            dma((2, 2, NE)),
            dma((2, 2, 2)),
            dma((2, 2, 2)),
            dma((2, 4, 2)),
            dma((2, 4, 2)),
            dma((8,)),
            dma((8,)),
            dma((2, 4)),
            dma((2, 4)),
            dma((2, 2)),
            dma((2, 2)),
            dma((2, 2, 2)),
            dma((2, 2, 2)),
            dma((3, NE)),
            dma((3, NE)),
        ],
        compiler_params=pltpu.CompilerParams(
            collective_id=0, has_side_effects=True, vmem_limit_bytes=62 * 1024 * 1024),
        cost_estimate=pl.CostEstimate(flops=16_000_000_000, bytes_accessed=22_000_000, transcendentals=1_000_000),
    )(
        tokens, out_grad, gates.T, labels.reshape(1, TD), text_picks, image_picks, block_mask,
        w_gate[0], w_up[0], w_down[0],
    )
    return input_grad, router_grad.T


def solution(mesh):
    placed = (
        P("expert", None),
        P("expert", None),
        P("expert", None),
        P("expert"),
        P(),
        P(),
        P("expert", "hidden"),
        P("expert", None, "hidden"),
        P("expert", None, "hidden"),
        P("expert", "hidden", None),
    )
    return jax.shard_map(
        body,
        mesh=mesh,
        in_specs=placed,
        out_specs=(P("expert", "hidden"), P("expert", None)),
        check_vma=False,
    )
```

time: 93.3 us -> 83.4 us (0.89)
  Pallas kernels: 87.5 us -> 79.5 us
  local copies, waits for them, and re-layouts: 4.85 us -> 3.08 us
    pallas_call x1, Pallas kernels: 87.5 us -> 79.5 us  [body(): pl.pallas_call(kernel, out_shape=(jax.ShapeDtypeStruct((TD, FB), BF16), j...]
    pallas_call x1 -> x0, local copies, waits for them, and re-layouts: 1.58 us -> none  [body(): pl.pallas_call(kernel, out_shape=(jax.ShapeDtypeStruct((TD, FB), BF16), j...]
where the time goes in v2:
time: 83.4 us; the launch traced here: 83.2 us
  Pallas kernels  79.5 us (95%)
  local copies, waits for them, and re-layouts  3.08 us (4%)
    pallas_call x1, Pallas kernels, body(): pl.pallas_call(kernel, out_shape=(jax.ShapeDtypeStruct((TD, FB), BF16), j...  79.5 us
    unnamed x2, local copies, waits for them, and re-layouts  3.08 us

profile of v2, /device:TPU:0, one launch (start us, length us, event | category | flops | bytes accessed | tf_op | source)
XLA Modules:
  0.0 83.2 jit_solution(264403060204015186)
XLA Ops:
  0.6 79.5 %shard_map.113 = (bf16[512,384]{1,0:T(8,128)(2,1)}, bf16[8,512]{1,0:T(8,128)(2,1)}) custom-call(bf16[512,3072]{1,0:T(8,128)(2,1)} %tok_h.1, bf16[512,3072]{1,0:T(8,128)(2,1)} %og_h.1, bf16[8,512]{1,0:T(8,128)(2,1)} %bitcast.10, s32[1,512]{1,0:T(1,128)} %bitcast.11, s32[8,512]{1,0:T(8,128)} %tpk.1, s32[8,256]{1,0:T(8,128)} %ipk.1, s32[1,8]{1,0:T(1,128)} %mask.1, ...), custom_call_target="tpu_custom_call" | custom-call | flops 16000000000 | bytes 22000000 | tf_op jit(solution)/shard_map/pallas_call | solution.py:628
  80.1 1.8 %copy.14 = bf16[512,384]{1,0:T(8,128)(2,1)} copy(bf16[512,384]{1,0:T(8,128)(2,1)} %get-tuple-element.8) | data formatting | bytes 786432
  81.9 1.3 %copy.15 = bf16[512,8]{0,1:T(8,128)(2,1)} copy(bf16[512,8]{0,1:T(8,128)(2,1)} %bitcast.6) | data formatting | bytes 16384

commit v3 on v2

--- a/solution.py
+++ b/solution.py
@@ -357,9 +357,9 @@
 
     pick_text(0, 1)
     pick_image(0)
-    left(0, 0)
     pick_text(1, 0)
     compact(0, 0, True)
+    left(0, 0)
     left(0, 1)
     pick_text(1, 1)
     pick_image(1)
@@ -377,9 +377,9 @@
     compact(1, 0, False)
     compact(1, 1, False)
     compact(1, 1, True)
-    project(0, 1)
     forward(1, 2)
     forward(1, 3)
+    project(0, 1)
     project(1, 1)
     project(1, 2)
     project(1, 3)
@@ -597,21 +597,21 @@
     finish_far(0)
     terms(0, 2)
     finish_free(0, 0)
-    terms(0, 3)
+    terms(1, 0)
     finish_free(0, 1)
-    terms(1, 0)
     finish_rest(0, 0)
     finish_rest(0, 1)
+    finish_far(1)
+    terms(0, 3)
     terms(1, 1)
-    finish_far(1)
+    send_scores()
     terms(1, 2)
     finish_free(1, 0)
-    terms(1, 3)
     finish_free(1, 1)
-    send_scores()
     finish_rest(1, 0)
     finish_rest(1, 1)
     send_rows(0)
+    terms(1, 3)
     flush()
     send_rows(1)
     scores_here()

time: 83.4 us -> 83.2 us (level)
  no operation moved by 1% of the time
where the time goes in v3:
time: 83.2 us; the launch traced here: 82.9 us
  Pallas kernels  79.2 us (95%)
  local copies, waits for them, and re-layouts  3.08 us (4%)
    pallas_call x1, Pallas kernels, body(): pl.pallas_call(kernel, out_shape=(jax.ShapeDtypeStruct((TD, FB), BF16), j...  79.2 us
    unnamed x2, local copies, waits for them, and re-layouts  3.08 us

profile of v3, /device:TPU:0, one launch (start us, length us, event | category | flops | bytes accessed | tf_op | source)
XLA Modules:
  0.0 82.9 jit_solution(12079462635164470931)
XLA Ops:
  0.6 79.2 %shard_map.113 = (bf16[512,384]{1,0:T(8,128)(2,1)}, bf16[8,512]{1,0:T(8,128)(2,1)}) custom-call(bf16[512,3072]{1,0:T(8,128)(2,1)} %tok_h.1, bf16[512,3072]{1,0:T(8,128)(2,1)} %og_h.1, bf16[8,512]{1,0:T(8,128)(2,1)} %bitcast.10, s32[1,512]{1,0:T(1,128)} %bitcast.11, s32[8,512]{1,0:T(8,128)} %tpk.1, s32[8,256]{1,0:T(8,128)} %ipk.1, s32[1,8]{1,0:T(1,128)} %mask.1, ...), custom_call_target="tpu_custom_call" | custom-call | flops 16000000000 | bytes 22000000 | tf_op jit(solution)/shard_map/pallas_call | solution.py:628
  79.9 1.8 %copy.14 = bf16[512,384]{1,0:T(8,128)(2,1)} copy(bf16[512,384]{1,0:T(8,128)(2,1)} %get-tuple-element.8) | data formatting | bytes 786432
  81.6 1.3 %copy.15 = bf16[512,8]{0,1:T(8,128)(2,1)} copy(bf16[512,8]{0,1:T(8,128)(2,1)} %bitcast.6) | data formatting | bytes 16384
